TPU v7x, 32 devices: a whole 2x2x4 slice. The times are simulated.
32 devices in a mesh: pack: 2 (over y), blk: 16 (over z, x, core).
Axes of the slice: x: 2, y: 2, z: 4, core: 2. Of those that a mesh axis runs over, the one named last changes fastest.
Arguments:
- frames: bfloat16 [4096, 1024], P(('pack', 'blk')), may hold values from -6 to 6
- skip_input: bfloat16 [4096, 1024], P(('pack', 'blk')), may hold values from -6 to 6
- lengths: int32 [2, 4], P('pack'), may hold values from 1 to 1856, as said below
- w_skip: bfloat16 [2048, 1024], P('blk')
- b_skip: bfloat16 [1024], P('blk'), may hold values from -3 to 3
- g_attn: bfloat16 [1024], P('blk'), may hold values from 0.5 to 1.5
- w_qkv: bfloat16 [1024, 3072], P('blk'), may hold values from -0.1875 to 0.1875
- w_out: bfloat16 [1024, 1024], P('blk'), may hold values from -1.5 to 1.5
- g_ff: bfloat16 [1024], P('blk'), may hold values from 0.5 to 1.5
- w_up: bfloat16 [1024, 4096], P('blk'), may hold values from -0.1875 to 0.1875
- b_up: bfloat16 [4096], P('blk'), may hold values from -3 to 3
- w_down: bfloat16 [4096, 1024], P('blk'), may hold values from -0.09375 to 0.09375
- b_down: bfloat16 [1024], P('blk'), may hold values from -3 to 3
- out_grad: bfloat16 [4096, 1024], P(('pack', 'blk')), may hold values from -6 to 6
Outputs:
- layer_out: bfloat16 [4096, 1024], P(('pack', 'blk'))
- frames_grad: bfloat16 [4096, 1024], P(('pack', 'blk'))
- skip_grad: bfloat16 [4096, 1024], P(('pack', 'blk'))
- w_skip_grad: float32 [2048, 1024], P('blk')
- b_skip_grad: float32 [1024], P('blk')
- g_attn_grad: float32 [1024], P('blk')
- w_qkv_grad: float32 [1024, 3072], P('blk')
- w_out_grad: float32 [1024, 1024], P('blk')
- g_ff_grad: float32 [1024], P('blk')
- w_up_grad: float32 [1024, 4096], P('blk')
- b_up_grad: float32 [4096], P('blk')
- w_down_grad: float32 [4096, 1024], P('blk')
- b_down_grad: float32 [1024], P('blk')
Inputs may be any that keep to these rules, and one draw needn't show every extreme that they name: Each row holds the 4 lengths of one pack in packing order and sums to 2048. One utterance, neither the first nor the last, at a place drawn from the seed, has 1856 frames; it starts within the first 128 frames of the pack and ends within the last 128. The other utterances together hold 192 frames, each fewer than 128.
All inputs are finite; a program needn't handle non-finite values.
Results may differ from a plain program's by a relative error of at most 0.018.
Values may be sent and summed in bfloat16 or wider, within the bound.
No kernel may reach another device: no remote copies, remote signals or barrier semaphores. Data moves between devices by JAX's collectives and lax.ppermute only.
A program may use at most 192 MiB of HBM per device.

v0:
```python
import math

import jax
import jax.numpy as jnp
from jax import lax
from jax.sharding import PartitionSpec as P

H = 16
HD = 64


EPSILON = 1e-06
MASKED_SCORE = -1e30


def passed_along(block, axis, distance):
    devices = range(lax.axis_size(axis))
    route = [((i - distance) % len(devices), i) for i in devices]
    return lax.ppermute(block, axis, route)


def normalize(stream, gain_vec):
    return stream * lax.rsqrt(jnp.mean(stream * stream, -1, keepdims=True) + EPSILON) * gain_vec


def activation(value):
    return jax.nn.gelu(value, approximate=True)


def rotate(tensor, offset, direction):
    half = tensor.shape[-1] // 2
    freq = 10000.0 ** (-(jnp.arange(half, dtype=jnp.float32) * 2.0 / tensor.shape[-1]))
    angle = offset.astype(jnp.float32)[:, None] * freq[None, :]
    cosine = jnp.cos(angle)[:, None, :]
    sine = direction * jnp.sin(angle)[:, None, :]
    first_half = tensor[..., :half]
    second_half = tensor[..., half:]
    return jnp.concatenate(
        [first_half * cosine - second_half * sine, second_half * cosine + first_half * sine], -1
    )


def segment_of(position, lengths_row):
    bounds = jnp.cumsum(lengths_row)
    after = position[:, None] >= bounds[None, :]
    segment = jnp.sum(after.astype(jnp.int32), 1, dtype=jnp.int32)
    before = jnp.sum(jnp.where(after, lengths_row[None, :], 0), 1, dtype=jnp.int32)
    return (segment, position - before)


def row_contract(left, right):
    return lax.dot_general(
        left, right, (((0,), (0,)), ((), ())), preferred_element_type=jnp.float32
    )


def times_transposed(left, right):
    return lax.dot_general(
        left, right, (((1,), (1,)), ((), ())), preferred_element_type=jnp.float32
    )


def local(
    frames,
    skip_input,
    lengths,
    w_skip,
    b_skip,
    g_attn,
    w_qkv,
    w_out,
    g_ff,
    w_up,
    b_up,
    w_down,
    b_down,
    out_grad,
):
    gathered = (
        lax.all_gather(w_skip, "blk", axis=0, tiled=True),
        lax.all_gather(b_skip, "blk", axis=0, tiled=True),
        lax.all_gather(g_attn, "blk", axis=0, tiled=True),
        lax.all_gather(w_qkv, "blk", axis=0, tiled=True),
        lax.all_gather(w_out, "blk", axis=0, tiled=True),
        lax.all_gather(g_ff, "blk", axis=0, tiled=True),
        lax.all_gather(w_up, "blk", axis=0, tiled=True),
        lax.all_gather(b_up, "blk", axis=0, tiled=True),
        lax.all_gather(w_down, "blk", axis=0, tiled=True),
        lax.all_gather(b_down, "blk", axis=0, tiled=True),
    )
    (
        skip_full,
        bias_skip,
        gain_attn,
        qkv_full,
        out_full,
        gain_ff,
        up_full,
        bias_up,
        down_full,
        bias_down,
    ) = gathered
    local_rows = frames.shape[0]
    model_width = frames.shape[1]
    score_scale = 1.0 / math.sqrt(HD)
    circle_size = lax.axis_size("blk")
    circle_index = lax.axis_index("blk")
    pack_lengths = lengths[0]
    row_numbers = jnp.arange(local_rows, dtype=jnp.int32)
    query_segment, offset = segment_of(circle_index * local_rows + row_numbers, pack_lengths)
    joined = jnp.concatenate([frames, skip_input], 1)
    stream_in = jnp.dot(joined, skip_full, preferred_element_type=jnp.float32) + bias_skip.astype(
        jnp.float32
    )
    attn_gain = gain_attn.astype(jnp.float32)
    normed_attn = normalize(stream_in, attn_gain).astype(jnp.bfloat16)
    projected = jnp.dot(normed_attn, qkv_full, preferred_element_type=jnp.float32)
    queries = rotate(projected[:, :model_width].reshape(local_rows, H, HD), offset, 1.0).astype(
        jnp.bfloat16
    )
    keys_local = (
        rotate(projected[:, model_width : 2 * model_width].reshape(local_rows, H, HD), offset, 1.0)
        .astype(jnp.bfloat16)
        .reshape(local_rows, model_width)
    )
    values_local = projected[:, 2 * model_width :].astype(jnp.bfloat16)
    row_max = jnp.full((H, local_rows), MASKED_SCORE, jnp.float32)
    keys_piece = lax.all_gather(keys_local, "blk", axis=0, tiled=True)
    values_piece = lax.all_gather(values_local, "blk", axis=0, tiled=True)
    key_count = keys_piece.shape[0]
    key_segment, _ = segment_of(jnp.arange(key_count, dtype=jnp.int32), pack_lengths)
    scores = (
        jnp.einsum(
            "qhd,khd->hqk",
            queries,
            keys_piece.reshape(key_count, H, HD),
            preferred_element_type=jnp.float32,
        )
        * score_scale
    )
    allowed = (query_segment[:, None] == key_segment[None, :])[None]
    scores = jnp.where(allowed, scores, MASKED_SCORE)
    new_max = jnp.maximum(row_max, jnp.max(scores, -1))
    weight = jnp.where(allowed, jnp.exp(scores - new_max[..., None]), 0.0)
    row_total = jnp.sum(weight, -1)
    weighted = jnp.einsum(
        "hqk,khd->hqd",
        weight.astype(jnp.bfloat16),
        values_piece.reshape(key_count, H, HD),
        preferred_element_type=jnp.float32,
    )
    row_max, row_total, weighted = (new_max, row_total, weighted)
    attn_heads = weighted / row_total[..., None]
    log_total = row_max + jnp.log(row_total)
    attn_rows = jnp.transpose(attn_heads, (1, 0, 2))
    attn_low = attn_rows.reshape(local_rows, model_width).astype(jnp.bfloat16)
    stream_mid = stream_in + jnp.dot(attn_low, out_full, preferred_element_type=jnp.float32)
    ff_gain = gain_ff.astype(jnp.float32)
    normed_ff = normalize(stream_mid, ff_gain).astype(jnp.bfloat16)
    hidden_pre = jnp.dot(normed_ff, up_full, preferred_element_type=jnp.float32) + bias_up.astype(
        jnp.float32
    )
    hidden_act = activation(hidden_pre).astype(jnp.bfloat16)
    layer_out = (
        stream_mid
        + jnp.dot(hidden_act, down_full, preferred_element_type=jnp.float32)
        + bias_down.astype(jnp.float32)
    ).astype(jnp.bfloat16)
    skip_full, qkv_full, out_full, up_full, down_full = (
        lax.all_gather(w_skip, "blk", axis=0, tiled=True),
        lax.all_gather(w_qkv, "blk", axis=0, tiled=True),
        lax.all_gather(w_out, "blk", axis=0, tiled=True),
        lax.all_gather(w_up, "blk", axis=0, tiled=True),
        lax.all_gather(w_down, "blk", axis=0, tiled=True),
    )
    act_grad = times_transposed(out_grad, down_full)
    _, gelu_back = jax.vjp(activation, hidden_pre)
    pre_grad = gelu_back(act_grad)[0].astype(jnp.bfloat16)
    grad_down = row_contract(hidden_act, out_grad)
    grad_bdown = jnp.sum(out_grad.astype(jnp.float32), 0)
    grad_up = row_contract(normed_ff, pre_grad)
    grad_bup = jnp.sum(pre_grad.astype(jnp.float32), 0)
    normed_ff_grad = times_transposed(pre_grad, up_full)
    _, norm_back_ff = jax.vjp(normalize, stream_mid, ff_gain)
    mid_norm_grad, grad_gff = norm_back_ff(normed_ff_grad)
    mid_grad = out_grad.astype(jnp.float32) + mid_norm_grad
    branch_grad = mid_grad.astype(jnp.bfloat16)
    grad_out = row_contract(attn_low, branch_grad)
    attn_grad = times_transposed(branch_grad, out_full).astype(jnp.bfloat16)
    attn_grad_heads = attn_grad.reshape(local_rows, H, HD)
    delta = jnp.einsum("qhd,hqd->hq", attn_grad_heads.astype(jnp.float32), attn_heads)

    def section(section_num, state_all):
        moving_kv, moving_grad, query_acc = state_all
        owner = (circle_index - section_num) % circle_size
        key_segment, _ = segment_of(owner * local_rows + row_numbers, pack_lengths)
        keys_flat = moving_kv[0]
        values_flat = moving_kv[1]
        keys_piece = keys_flat.reshape(local_rows, H, HD)
        values_piece = values_flat.reshape(local_rows, H, HD)
        scores = (
            jnp.einsum("qhd,khd->hqk", queries, keys_piece, preferred_element_type=jnp.float32)
            * score_scale
        )
        allowed = (query_segment[:, None] == key_segment[None, :])[None]
        probs = jnp.where(allowed, jnp.exp(scores - log_total[..., None]), 0.0)
        probs_low = probs.astype(jnp.bfloat16)
        prob_grad = jnp.einsum(
            "qhd,khd->hqk", attn_grad_heads, values_piece, preferred_element_type=jnp.float32
        )
        score_grad = (probs * (prob_grad - delta[..., None])).astype(jnp.bfloat16)
        query_acc = (
            query_acc
            + jnp.einsum("hqk,khd->qhd", score_grad, keys_piece, preferred_element_type=jnp.float32)
            * score_scale
        )
        key_part = (
            jnp.einsum("hqk,qhd->khd", score_grad, queries, preferred_element_type=jnp.float32)
            * score_scale
        )
        value_part = jnp.einsum(
            "hqk,qhd->khd", probs_low, attn_grad_heads, preferred_element_type=jnp.float32
        )
        moving_grad = moving_grad + jnp.stack(
            [key_part.reshape(local_rows, model_width), value_part.reshape(local_rows, model_width)]
        )
        moving_kv = passed_along(moving_kv, "blk", 1)
        moving_grad = passed_along(moving_grad.astype(jnp.bfloat16), "blk", 1).astype(
            moving_grad.dtype
        )
        return (moving_kv, moving_grad, query_acc)

    kv_start = jnp.stack([keys_local, values_local])
    circle_start = (
        kv_start,
        jnp.zeros((2, local_rows, model_width), jnp.float32),
        jnp.zeros((local_rows, H, HD), jnp.float32),
    )
    _, kv_grad, query_grad = lax.fori_loop(0, circle_size, section, circle_start)
    query_raw = rotate(query_grad, offset, -1.0).reshape(local_rows, model_width)
    key_raw = rotate(kv_grad[0].reshape(local_rows, H, HD), offset, -1.0).reshape(
        local_rows, model_width
    )
    projected_grad = jnp.concatenate([query_raw, key_raw, kv_grad[1]], 1).astype(jnp.bfloat16)
    grad_qkv = row_contract(normed_attn, projected_grad)
    normed_attn_grad = times_transposed(projected_grad, qkv_full)
    _, norm_back_attn = jax.vjp(normalize, stream_in, attn_gain)
    in_norm_grad, grad_gattn = norm_back_attn(normed_attn_grad)
    in_low = (mid_grad + in_norm_grad).astype(jnp.bfloat16)
    grad_skip = row_contract(joined, in_low)
    grad_bskip = jnp.sum(in_low.astype(jnp.float32), 0)
    joined_grad = times_transposed(in_low, skip_full)
    frames_grad = joined_grad[:, :model_width].astype(jnp.bfloat16)
    skip_grad = joined_grad[:, model_width:].astype(jnp.bfloat16)
    shares = (
        lax.psum_scatter(
            grad_skip.astype(jnp.bfloat16), "blk", scatter_dimension=0, tiled=True
        ).astype(jnp.float32),
        lax.psum_scatter(
            grad_bskip.astype(jnp.bfloat16), "blk", scatter_dimension=0, tiled=True
        ).astype(jnp.float32),
        lax.psum_scatter(
            grad_gattn.astype(jnp.bfloat16), "blk", scatter_dimension=0, tiled=True
        ).astype(jnp.float32),
        lax.psum_scatter(
            grad_qkv.astype(jnp.bfloat16), "blk", scatter_dimension=0, tiled=True
        ).astype(jnp.float32),
        lax.psum_scatter(
            grad_out.astype(jnp.bfloat16), "blk", scatter_dimension=0, tiled=True
        ).astype(jnp.float32),
        lax.psum_scatter(
            grad_gff.astype(jnp.bfloat16), "blk", scatter_dimension=0, tiled=True
        ).astype(jnp.float32),
        lax.psum_scatter(
            grad_up.astype(jnp.bfloat16), "blk", scatter_dimension=0, tiled=True
        ).astype(jnp.float32),
        lax.psum_scatter(
            grad_bup.astype(jnp.bfloat16), "blk", scatter_dimension=0, tiled=True
        ).astype(jnp.float32),
        lax.psum_scatter(
            grad_down.astype(jnp.bfloat16), "blk", scatter_dimension=0, tiled=True
        ).astype(jnp.float32),
        lax.psum_scatter(
            grad_bdown.astype(jnp.bfloat16), "blk", scatter_dimension=0, tiled=True
        ).astype(jnp.float32),
    )
    summed = tuple(
        (
            lax.psum(shares[0].astype(jnp.bfloat16), "pack").astype(jnp.float32),
            lax.psum(shares[1].astype(jnp.bfloat16), "pack").astype(jnp.float32),
            lax.psum(shares[2].astype(jnp.bfloat16), "pack").astype(jnp.float32),
            lax.psum(shares[3].astype(jnp.bfloat16), "pack").astype(jnp.float32),
            lax.psum(shares[4].astype(jnp.bfloat16), "pack").astype(jnp.float32),
            lax.psum(shares[5].astype(jnp.bfloat16), "pack").astype(jnp.float32),
            lax.psum(shares[6].astype(jnp.bfloat16), "pack").astype(jnp.float32),
            lax.psum(shares[7].astype(jnp.bfloat16), "pack").astype(jnp.float32),
            lax.psum(shares[8].astype(jnp.bfloat16), "pack").astype(jnp.float32),
            lax.psum(shares[9].astype(jnp.bfloat16), "pack").astype(jnp.float32),
        )
    )
    return (
        layer_out,
        frames_grad,
        skip_grad,
        summed[0],
        summed[1],
        summed[2],
        summed[3],
        summed[4],
        summed[5],
        summed[6],
        summed[7],
        summed[8],
        summed[9],
    )


def solution(mesh):
    return jax.shard_map(
        local,
        mesh=mesh,
        in_specs=(
            P(("pack", "blk"), None),
            P(("pack", "blk"), None),
            P("pack", None),
            P("blk", None),
            P("blk"),
            P("blk"),
            P("blk", None),
            P("blk", None),
            P("blk"),
            P("blk", None),
            P("blk"),
            P("blk", None),
            P("blk"),
            P(("pack", "blk"), None),
        ),
        out_specs=(
            P(("pack", "blk"), None),
            P(("pack", "blk"), None),
            P(("pack", "blk"), None),
            P("blk", None),
            P("blk"),
            P("blk"),
            P("blk", None),
            P("blk", None),
            P("blk"),
            P("blk", None),
            P("blk"),
            P("blk", None),
            P("blk"),
        ),
        check_vma=False,
    )
```

profile of v0, /device:TPU:0, one launch (start us, length us, event | category | flops | bytes accessed | tf_op | source)
XLA Modules:
  0.0 1296.9 jit_solution(15484826476267364698)
XLA Ops:
  14.0 36.1 %all-reduce.10 = (bf16[1024]{0:T(1024)(128)(2,1)S(1)}, bf16[1024]{0:T(1024)(128)(2,1)S(1)}, bf16[1024]{0:T(1024)(128)(2,1)S(1)}) all-reduce(bf16[1024]{0:T(1024)(128)(2,1)S(1)} %dynamic-update-slice, bf16[1024]{0:T(1024)(128)(2,1)S(1)} %dynamic-update-slice.1, ...), channel_id=1, replica_groups=mesh['pack'=2,'blk'=16] {'blk'}, use_global_device_ids=true, to_apply=%add | all-reduce | flops 3072 | bytes 12288
  52.1 11.6 all-gather.9.cloned.1.call-done
  66.7 59.8 %all-gather.11.cloned.1.call-done = bf16[1024,3072]{1,0:T(8,128)(2,1)} async-done(((bf16[64,3072]{1,0:T(8,128)(2,1)}), bf16[1024,3072]{1,0:T(8,128)(2,1)}) %all-gather.11.cloned.1.call-update) | async-done | bytes 6291472 | tf_op jit(solution)/shard_map/all_gather | solution.py:83
  135.1 19.3 %all-gather = bf16[16,1,256]{2,1,0:T(2,128)(2,1)S(1)} all-gather(bf16[1,1,256]{2,1,0:T(2,128)(2,1)S(1)} %reshape.336), channel_id=1, replica_groups=mesh['pack'=2,'blk'=16] {'blk'}, dimensions={0}, use_global_device_ids=true | all-gather | bytes 8704 | tf_op jit(solution)/shard_map/all_gather | solution.py:87
  161.5 40.8 %all-gather.21.cloned.1.call-done = bf16[4096,1024]{1,0:T(8,128)(2,1)} async-done(((bf16[256,1024]{1,0:T(8,128)(2,1)}), bf16[4096,1024]{1,0:T(8,128)(2,1)}) %all-gather.21.cloned.1.call-update) | async-done | bytes 8388624 | tf_op jit(solution)/shard_map/all_gather | solution.py:88
  209.8 43.9 %all-gather.15.cloned.1.call-done = bf16[2048,1024]{1,0:T(8,128)(2,1)} async-done(((bf16[128,1024]{1,0:T(8,128)(2,1)}), bf16[2048,1024]{1,0:T(8,128)(2,1)}) %all-gather.15.cloned.1.call-update) | async-done | bytes 4194320 | tf_op jit(solution)/shard_map/all_gather | solution.py:129
  260.2 47.9 %all-gather.13.cloned.1.call-done = bf16[2048,1024]{0,1:T(8,128)(2,1)} async-done(((bf16[128,1024]{0,1:T(8,128)(2,1)}), bf16[2048,1024]{0,1:T(8,128)(2,1)}) %all-gather.13.cloned.1.call-update) | async-done | bytes 4194320 | tf_op jit(solution)/shard_map/all_gather | solution.py:128
  318.6 12.0 fusion.31
  330.6 19.1 %all-gather.17.cloned.1.call-done = bf16[1024,1024]{1,0:T(8,128)(2,1)} async-done(((bf16[64,1024]{1,0:T(8,128)(2,1)}), bf16[1024,1024]{1,0:T(8,128)(2,1)}) %all-gather.17.cloned.1.call-update) | async-done | bytes 2097168 | tf_op jit(solution)/shard_map/all_gather | solution.py:84
  351.9 73.7 %all-gather.19.cloned.1.call-done = bf16[1024,4096]{1,0:T(8,128)(2,1)} async-done(((bf16[64,4096]{1,0:T(8,128)(2,1)}), bf16[1024,4096]{1,0:T(8,128)(2,1)}) %all-gather.19.cloned.1.call-update) | async-done | bytes 8388624 | tf_op jit(solution)/shard_map/all_gather | solution.py:86
  442.0 374.2 %while.20 = (s32[]{:T(128)}, bf16[2,128,1024]{1,2,0:T(8,128)(2,1)}, f32[2,128,1024]{1,2,0:T(8,128)S(1)}, f32[128,16,64]{0,2,1:T(8,128)}, s32[128]{0:T(128)S(1)},...) while((s32[]{:T(128)}, bf16[2,128,1024]{1,2,0:T(8,128)(2,1)}, ...), condition=%wide.region_12.13_spmd.clone, body=%wide.region_10.12_spmd.clone.sunk | while | flops 171460112 | bytes 19188616 | solution.py:239
  449.9 9.7 collective-permute-done.1
  473.2 13.1 %collective-permute-done.1 = bf16[2,128,1024]{1,2,0:T(8,128)(2,1)} collective-permute-done((bf16[2,128,1024]{1,2,0:T(8,128)(2,1)}, bf16[2,128,1024]{1,2,0:T(8,128)(2,1)}, u32[]{:S(2)}, u32[]{:S(2)}) %collective-permute-start.1) | collective-permute-done | bytes 524320 | tf_op jit(solution)/shard_map/while/body/eval_jaxpr/ppermute | solution.py:19
  501.7 10.5 collective-permute-done.1
  525.9 9.3 collective-permute-done.1
  571.8 9.3 collective-permute-done.1
  617.7 9.3 collective-permute-done.1
  709.4 9.3 collective-permute-done.1
  801.2 9.3 collective-permute-done.1
  846.5 50.8 %reduce-scatter.6.cloned.1.call-done = bf16[128,1024]{1,0:T(8,128)(2,1)} async-done(((bf16[2048,1024]{1,0:T(8,128)(2,1)}), bf16[128,1024]{1,0:T(8,128)(2,1)}) %reduce-scatter.6.cloned.1.call-update) | async-done | bytes 262160 | tf_op jit(solution)/shard_map/reduce_scatter | solution.py:256
  897.3 87.9 %reduce-scatter.8.cloned.1.call-done = bf16[64,3072]{1,0:T(8,128)(2,1)} async-done(((bf16[1024,3072]{1,0:T(8,128)(2,1)}), bf16[64,3072]{1,0:T(8,128)(2,1)}) %reduce-scatter.8.cloned.1.call-update) | async-done | bytes 393232 | tf_op jit(solution)/shard_map/reduce_scatter | solution.py:265
  985.1 108.5 %reduce-scatter.12.cloned.1.call-done = bf16[64,4096]{1,0:T(8,128)(2,1)} async-done(((bf16[1024,4096]{1,0:T(8,128)(2,1)}), bf16[64,4096]{1,0:T(8,128)(2,1)}) %reduce-scatter.12.cloned.1.call-update) | async-done | bytes 524304 | tf_op jit(solution)/shard_map/reduce_scatter | solution.py:274
  1093.6 108.8 %reduce-scatter.14.cloned.1.call-done = bf16[256,1024]{1,0:T(8,128)(2,1)} async-done(((bf16[4096,1024]{1,0:T(8,128)(2,1)}), bf16[256,1024]{1,0:T(8,128)(2,1)}) %reduce-scatter.14.cloned.1.call-update) | async-done | bytes 524304 | tf_op jit(solution)/shard_map/reduce_scatter | solution.py:280
  1204.0 60.2 %all-reduce.9 = (bf16[1024]{0:T(1024)(128)(2,1)S(1)}, bf16[1024]{0:T(1024)(128)(2,1)S(1)}, bf16[1024]{0:T(1024)(128)(2,1)S(1)}, bf16[1024]{0:T(1024)(128)(2,1)S(...) all-reduce(bf16[1024]{0:T(1024)(128)(2,1)S(1)} %dynamic-update-slic, ...), channel_id=1, replica_groups=mesh['pack'=2,'blk'=16] {'blk'}, use_global_device_ids=true, to_apply=%add.3 | all-reduce | flops 9216 | bytes 36864
  (406 shorter events, 419.0 us)
Async XLA Ops:
  7.2 56.5 %all-gather.9.cloned.1.call-start = ((), (), s32[]{:S(2)}) async-start(), calls=%async_computation.5 | async-start | bytes 4456448 | tf_op jit(solution)/shard_map/all_gather | solution.py:80
  7.9 118.6 %all-gather.11.cloned.1.call-start = ((), (), s32[]{:S(2)}) async-start(), calls=%async_computation.6 | async-start | bytes 6684672 | tf_op jit(solution)/shard_map/all_gather | solution.py:83
  8.7 193.6 %all-gather.21.cloned.1.call-start = ((), (), s32[]{:S(2)}) async-start(), calls=%async_computation.11 | async-start | bytes 8912896 | tf_op jit(solution)/shard_map/all_gather | solution.py:88
  9.4 244.3 %all-gather.15.cloned.1.call-start = ((), (), s32[]{:S(2)}) async-start(), calls=%async_computation.8 | async-start | bytes 4456448 | tf_op jit(solution)/shard_map/all_gather | solution.py:129
  131.1 176.9 %all-gather.13.cloned.1.call-start = ((), (), s32[]{:S(2)}) async-start(), calls=%async_computation.7 | async-start | bytes 4456448 | tf_op jit(solution)/shard_map/all_gather | solution.py:128
  133.5 216.2 %all-gather.17.cloned.1.call-start = ((), (), s32[]{:S(2)}) async-start(), calls=%async_computation.9 | async-start | bytes 2228224 | tf_op jit(solution)/shard_map/all_gather | solution.py:84
  134.1 291.5 %all-gather.19.cloned.1.call-start = ((), (), s32[]{:S(2)}) async-start(), calls=%async_computation.10 | async-start | bytes 8912896 | tf_op jit(solution)/shard_map/all_gather | solution.py:86
  134.8 711.6 %reduce-scatter.10.cloned.1.call-start = ((), (), s32[]{:S(2)}) async-start(), calls=%async_computation.14 | async-start | bytes 2228224 | tf_op jit(solution)/shard_map/reduce_scatter | solution.py:268
  441.8 455.4 %reduce-scatter.6.cloned.1.call-start = ((), (), s32[]{:S(2)}) async-start(), calls=%async_computation.12 | async-start | bytes 4456448 | tf_op jit(solution)/shard_map/reduce_scatter | solution.py:256
  470.9 22.9 %collective-permute-start = (bf16[2,128,1024]{1,2,0:T(8,128)(2,1)S(1)}, bf16[2,128,1024]{1,2,0:T(8,128)(2,1)}, u32[]{:S(2)}, u32[]{:S(2)}) collective-permute-start(bf16[2,128,1024]{1,2,0:T(8,128)(2,1)S(1)} %copy.71), channel_id=1, source_target_pairs={{15,0},{0,1},{1,2},{2,3},{3,4},{4,5},{5,6},{6,7},{7,8},{8,9},{9,10... | collective-permute-start | bytes 1572872 | tf_op jit(solution)/shard_map/while/body/eval_jaxpr/ppermute | solution.py:19
  499.4 18.5 %collective-permute-start = (bf16[2,128,1024]{1,2,0:T(8,128)(2,1)S(1)}, bf16[2,128,1024]{1,2,0:T(8,128)(2,1)}, u32[]{:S(2)}, u32[]{:S(2)}) collective-permute-start(bf16[2,128,1024]{1,2,0:T(8,128)(2,1)S(1)} %copy.71), channel_id=1, source_target_pairs={{15,0},{0,1},{1,2},{2,3},{3,4},{4,5},{5,6},{6,7},{7,8},{8,9},{9,10... | collective-permute-start | bytes 1572872 | tf_op jit(solution)/shard_map/while/body/eval_jaxpr/ppermute | solution.py:19
  523.6 17.2 %collective-permute-start = (bf16[2,128,1024]{1,2,0:T(8,128)(2,1)S(1)}, bf16[2,128,1024]{1,2,0:T(8,128)(2,1)}, u32[]{:S(2)}, u32[]{:S(2)}) collective-permute-start(bf16[2,128,1024]{1,2,0:T(8,128)(2,1)S(1)} %copy.71), channel_id=1, source_target_pairs={{15,0},{0,1},{1,2},{2,3},{3,4},{4,5},{5,6},{6,7},{7,8},{8,9},{9,10... | collective-permute-start | bytes 1572872 | tf_op jit(solution)/shard_map/while/body/eval_jaxpr/ppermute | solution.py:19
  546.6 17.2 %collective-permute-start = (bf16[2,128,1024]{1,2,0:T(8,128)(2,1)S(1)}, bf16[2,128,1024]{1,2,0:T(8,128)(2,1)}, u32[]{:S(2)}, u32[]{:S(2)}) collective-permute-start(bf16[2,128,1024]{1,2,0:T(8,128)(2,1)S(1)} %copy.71), channel_id=1, source_target_pairs={{15,0},{0,1},{1,2},{2,3},{3,4},{4,5},{5,6},{6,7},{7,8},{8,9},{9,10... | collective-permute-start | bytes 1572872 | tf_op jit(solution)/shard_map/while/body/eval_jaxpr/ppermute | solution.py:19
  569.5 17.2 %collective-permute-start = (bf16[2,128,1024]{1,2,0:T(8,128)(2,1)S(1)}, bf16[2,128,1024]{1,2,0:T(8,128)(2,1)}, u32[]{:S(2)}, u32[]{:S(2)}) collective-permute-start(bf16[2,128,1024]{1,2,0:T(8,128)(2,1)S(1)} %copy.71), channel_id=1, source_target_pairs={{15,0},{0,1},{1,2},{2,3},{3,4},{4,5},{5,6},{6,7},{7,8},{8,9},{9,10... | collective-permute-start | bytes 1572872 | tf_op jit(solution)/shard_map/while/body/eval_jaxpr/ppermute | solution.py:19
  592.4 17.2 %collective-permute-start = (bf16[2,128,1024]{1,2,0:T(8,128)(2,1)S(1)}, bf16[2,128,1024]{1,2,0:T(8,128)(2,1)}, u32[]{:S(2)}, u32[]{:S(2)}) collective-permute-start(bf16[2,128,1024]{1,2,0:T(8,128)(2,1)S(1)} %copy.71), channel_id=1, source_target_pairs={{15,0},{0,1},{1,2},{2,3},{3,4},{4,5},{5,6},{6,7},{7,8},{8,9},{9,10... | collective-permute-start | bytes 1572872 | tf_op jit(solution)/shard_map/while/body/eval_jaxpr/ppermute | solution.py:19
  615.4 17.2 %collective-permute-start = (bf16[2,128,1024]{1,2,0:T(8,128)(2,1)S(1)}, bf16[2,128,1024]{1,2,0:T(8,128)(2,1)}, u32[]{:S(2)}, u32[]{:S(2)}) collective-permute-start(bf16[2,128,1024]{1,2,0:T(8,128)(2,1)S(1)} %copy.71), channel_id=1, source_target_pairs={{15,0},{0,1},{1,2},{2,3},{3,4},{4,5},{5,6},{6,7},{7,8},{8,9},{9,10... | collective-permute-start | bytes 1572872 | tf_op jit(solution)/shard_map/while/body/eval_jaxpr/ppermute | solution.py:19
  638.3 17.2 %collective-permute-start = (bf16[2,128,1024]{1,2,0:T(8,128)(2,1)S(1)}, bf16[2,128,1024]{1,2,0:T(8,128)(2,1)}, u32[]{:S(2)}, u32[]{:S(2)}) collective-permute-start(bf16[2,128,1024]{1,2,0:T(8,128)(2,1)S(1)} %copy.71), channel_id=1, source_target_pairs={{15,0},{0,1},{1,2},{2,3},{3,4},{4,5},{5,6},{6,7},{7,8},{8,9},{9,10... | collective-permute-start | bytes 1572872 | tf_op jit(solution)/shard_map/while/body/eval_jaxpr/ppermute | solution.py:19
  661.3 17.2 %collective-permute-start = (bf16[2,128,1024]{1,2,0:T(8,128)(2,1)S(1)}, bf16[2,128,1024]{1,2,0:T(8,128)(2,1)}, u32[]{:S(2)}, u32[]{:S(2)}) collective-permute-start(bf16[2,128,1024]{1,2,0:T(8,128)(2,1)S(1)} %copy.71), channel_id=1, source_target_pairs={{15,0},{0,1},{1,2},{2,3},{3,4},{4,5},{5,6},{6,7},{7,8},{8,9},{9,10... | collective-permute-start | bytes 1572872 | tf_op jit(solution)/shard_map/while/body/eval_jaxpr/ppermute | solution.py:19
  684.2 17.2 %collective-permute-start = (bf16[2,128,1024]{1,2,0:T(8,128)(2,1)S(1)}, bf16[2,128,1024]{1,2,0:T(8,128)(2,1)}, u32[]{:S(2)}, u32[]{:S(2)}) collective-permute-start(bf16[2,128,1024]{1,2,0:T(8,128)(2,1)S(1)} %copy.71), channel_id=1, source_target_pairs={{15,0},{0,1},{1,2},{2,3},{3,4},{4,5},{5,6},{6,7},{7,8},{8,9},{9,10... | collective-permute-start | bytes 1572872 | tf_op jit(solution)/shard_map/while/body/eval_jaxpr/ppermute | solution.py:19
  707.1 17.2 %collective-permute-start = (bf16[2,128,1024]{1,2,0:T(8,128)(2,1)S(1)}, bf16[2,128,1024]{1,2,0:T(8,128)(2,1)}, u32[]{:S(2)}, u32[]{:S(2)}) collective-permute-start(bf16[2,128,1024]{1,2,0:T(8,128)(2,1)S(1)} %copy.71), channel_id=1, source_target_pairs={{15,0},{0,1},{1,2},{2,3},{3,4},{4,5},{5,6},{6,7},{7,8},{8,9},{9,10... | collective-permute-start | bytes 1572872 | tf_op jit(solution)/shard_map/while/body/eval_jaxpr/ppermute | solution.py:19
  826.9 158.2 %reduce-scatter.8.cloned.1.call-start = ((), (), s32[]{:S(2)}) async-start(), calls=%async_computation.13 | async-start | bytes 6684672 | tf_op jit(solution)/shard_map/reduce_scatter | solution.py:265
  831.7 261.9 %reduce-scatter.12.cloned.1.call-start = ((), (), s32[]{:S(2)}) async-start(), calls=%async_computation.15 | async-start | bytes 8912896 | tf_op jit(solution)/shard_map/reduce_scatter | solution.py:274
  838.8 363.6 %reduce-scatter.14.cloned.1.call-start = ((), (), s32[]{:S(2)}) async-start(), calls=%async_computation.16 | async-start | bytes 8912896 | tf_op jit(solution)/shard_map/reduce_scatter | solution.py:280
  846.1 436.2 %all-reduce.15.cloned.1.call-start = ((), (), s32[]{:S(2)}) async-start(), calls=%async_computation.17 | async-start | bytes 3670016 | tf_op jit(solution)/shard_map/psum | solution.py:289
  (41 other events, 835.6 us)
Sparse Core Ops, SparseCore 0:
  10.2 53.4 all-gather.8
  65.9 60.4 all-gather.10
  128.6 73.5 all-gather.20
  204.9 48.7 all-gather.14
  256.3 51.7 all-gather.12
  310.0 39.6 all-gather.16
  351.9 73.6 all-gather.18
  441.9 65.8 reduce-scatter.9
  827.1 70.1 reduce-scatter.5
  901.0 84.0 reduce-scatter.7
  989.7 103.7 reduce-scatter.11
  1098.0 104.3 reduce-scatter.13
  1205.1 57.6 all-reduce.14
where the time goes:
time: 1310 us; the launch traced here: 1300 us
  waiting for transfers between devices  884 us (67%)
  matrix products  175 us (13%)
  blocking collectives  121 us (9%)
  other arithmetic  56 us (4%)
  local copies, waits for them, and re-layouts  42.3 us (3%)
  between operations  16.7 us (1%)
    ppermute x32, waiting for transfers between devices, passed_along(): return lax.ppermute(block, axis, route)  228 us
    reduce_scatter x1, waiting for transfers between devices, local(): lax.psum_scatter(grad_down.astype(jnp.bfloat16), 'blk', scatter_dimension...  109 us
    reduce_scatter x1, waiting for transfers between devices, local(): lax.psum_scatter(grad_up.astype(jnp.bfloat16), 'blk', scatter_dimension=0...  108 us
    unnamed x2, blocking collectives  96.4 us
    reduce_scatter x1, waiting for transfers between devices, local(): lax.psum_scatter(grad_qkv.astype(jnp.bfloat16), 'blk', scatter_dimension=...  87.9 us
    all_gather x1, waiting for transfers between devices, local(): lax.all_gather(w_up, 'blk', axis=0, tiled=True)  73.7 us
    all_gather x1, waiting for transfers between devices, local(): lax.all_gather(w_qkv, 'blk', axis=0, tiled=True)  59.8 us
    reduce_scatter x1, waiting for transfers between devices, local(): lax.psum_scatter(grad_skip.astype(jnp.bfloat16), 'blk', scatter_dimension...  50.8 us
  transfers between devices with their start and end apart: 45, of which 43 were waited for; matrix products, arithmetic and copies ran while one was open for 19% of the time, Pallas kernels for 0%

commit v1 on v0

v1 whole, which is shorter than its diff:
```python
import functools
import math

import jax
import jax.numpy as jnp
from jax import lax
from jax.experimental import pallas as pl
from jax.experimental.pallas import tpu as pltpu
from jax.sharding import PartitionSpec as P

H = 16
HD = 64
EPSILON = 1e-06
MASKED_SCORE = -1e30
ROWS = 128
VMEM = 56 * 1024 * 1024
BF = jnp.bfloat16
F32 = jnp.float32


def mm(left, right):
    return jnp.dot(left, right, preferred_element_type=F32)


def mm_nt(left, right):
    return lax.dot_general(left, right, (((1,), (1,)), ((), ())), preferred_element_type=F32)


def mm_tn(left, right):
    return lax.dot_general(left, right, (((0,), (0,)), ((), ())), preferred_element_type=F32)


def whole(shape):
    return pl.BlockSpec(shape, lambda *_: (0,) * len(shape))


def segment_of(position, lengths_row):
    bounds = jnp.cumsum(lengths_row)
    after = position[:, None] >= bounds[None, :]
    segment = jnp.sum(after.astype(jnp.int32), 1, dtype=jnp.int32)
    before = jnp.sum(jnp.where(after, lengths_row[None, :], 0), 1, dtype=jnp.int32)
    return segment, position - before


def angles(offset):
    freq = 10000.0 ** (-(jnp.arange(HD // 2, dtype=F32) * 2.0 / HD))
    angle = offset.astype(F32)[:, None] * freq[None, :]
    return jnp.cos(angle), jnp.sin(angle)


def activation(value):
    return jax.nn.gelu(value, approximate=True)


def pack_pair(block, lane_low):
    half = block.shape[0] // 2
    top, bottom = block[:half], block[half:]
    even = jnp.where(lane_low, top, pltpu.roll(bottom, HD, 1))
    odd = jnp.where(lane_low, pltpu.roll(top, HD, 1), bottom)
    return even, odd


def rope_pack_kernel(proj_ref, cos_ref, sin_ref, out_ref):
    rows = proj_ref.shape[0]
    lane = lax.broadcasted_iota(jnp.int32, (rows, 128), 1)
    first = (lane % HD) < HD // 2
    lane_low = lane[: rows // 2] < HD
    cosine, sine = cos_ref[...], sin_ref[...]
    for part in range(3):
        for pair in range(H // 2):
            at = (part * H + 2 * pair) * HD
            block = proj_ref[:, at : at + 128]
            if part < 2:
                swapped = jnp.where(first, pltpu.roll(block, 128 - HD // 2, 1), pltpu.roll(block, HD // 2, 1))
                block = block * cosine + swapped * sine
            block = block.astype(BF).astype(F32)
            if part == 0:
                block = block * (1.0 / math.sqrt(HD))
            even, odd = pack_pair(block, lane_low)
            out_ref[2 * pair, part] = even.astype(BF)
            out_ref[2 * pair + 1, part] = odd.astype(BF)


def rope_pack(proj, cos_pair, sin_pair):
    rows = proj.shape[0]
    return pl.pallas_call(
        rope_pack_kernel,
        out_shape=jax.ShapeDtypeStruct((H, 3, rows // 2, 128), BF),
        compiler_params=pltpu.CompilerParams(vmem_limit_bytes=VMEM),
        name="rope_pack",
    )(proj, cos_pair, sin_pair)


def pack_kernel(in_ref, out_ref):
    rows = in_ref.shape[0]
    lane_low = lax.broadcasted_iota(jnp.int32, (rows // 2, 128), 1) < HD
    for pair in range(H // 2):
        even, odd = pack_pair(in_ref[:, pair * 128 : pair * 128 + 128].astype(F32), lane_low)
        out_ref[2 * pair] = even.astype(BF)
        out_ref[2 * pair + 1] = odd.astype(BF)


def pack_heads(rows_all):
    return pl.pallas_call(
        pack_kernel,
        out_shape=jax.ShapeDtypeStruct((H, rows_all.shape[0] // 2, 128), BF),
        compiler_params=pltpu.CompilerParams(vmem_limit_bytes=VMEM),
        name="pack_heads",
    )(rows_all)


def unpack_kernel(in_ref, out_ref):
    parts, half = in_ref.shape[1], in_ref.shape[2]
    lane_low = lax.broadcasted_iota(jnp.int32, (half, 128), 1) < HD
    for part in range(parts):
        for pair in range(H // 2):
            even = in_ref[2 * pair, part].astype(F32)
            odd = in_ref[2 * pair + 1, part].astype(F32)
            top = jnp.where(lane_low, even, pltpu.roll(odd, HD, 1))
            bottom = jnp.where(lane_low, pltpu.roll(even, HD, 1), odd)
            at = (part * H + 2 * pair) * HD
            out_ref[:half, at : at + 128] = top.astype(BF)
            out_ref[half:, at : at + 128] = bottom.astype(BF)


def unpack_heads(packed):
    _, parts, half, _ = packed.shape
    return pl.pallas_call(
        unpack_kernel,
        out_shape=jax.ShapeDtypeStruct((2 * half, parts * H * HD), BF),
        compiler_params=pltpu.CompilerParams(vmem_limit_bytes=VMEM),
        name="unpack_heads",
    )(packed)


def unpack_all(src_ref, part, dst_ref, steps):
    half = src_ref.shape[-2]
    each = ROWS // half
    for g in range(steps):
        block = src_ref[g * each : (g + 1) * each, part].reshape(ROWS, 128).astype(F32)
        dst_ref[g * 2 * ROWS : g * 2 * ROWS + ROWS] = block[:, :HD].astype(dst_ref.dtype)
        dst_ref[g * 2 * ROWS + ROWS : (g + 1) * 2 * ROWS] = block[:, HD:].astype(dst_ref.dtype)


def attend_kernel(qkv_ref, segc_ref, segr_ref, out_ref, attn_ref, lse_ref, q_s, k_s, v_s, vt_s):
    g = pl.program_id(0)
    steps = pl.num_programs(0)
    half = qkv_ref.shape[-2]
    each = ROWS // half

    @pl.when(g == 0)
    def _():
        total = q_s.shape[0] // (2 * ROWS)
        unpack_all(qkv_ref, 0, q_s, total)
        unpack_all(qkv_ref, 1, k_s, total)
        unpack_all(qkv_ref, 2, v_s, total)
        vt_s[...] = jnp.transpose(v_s[...].astype(F32)).astype(BF)

    at = pl.multiple_of(g * 2 * ROWS, 2 * ROWS)
    scores = mm_nt(k_s[...], q_s[pl.ds(at, 2 * ROWS)])
    allowed = segc_ref[...] == segr_ref[:, pl.ds(at, 2 * ROWS)]
    scores = jnp.where(allowed, scores, MASKED_SCORE)
    top = jnp.max(scores, 0, keepdims=True)
    weight = jnp.exp(scores - top)
    total = jnp.sum(weight, 0, keepdims=True)
    attn_t = mm(vt_s[...], weight.astype(BF)) / total
    attn_ref[:, pl.ds(at, 2 * ROWS)] = attn_t
    lse_ref[:, pl.ds(at, 2 * ROWS)] = top + jnp.log(total)
    rows = jnp.transpose(attn_t)
    joined = jnp.concatenate([rows[:ROWS], rows[ROWS:]], 1).astype(BF)
    out_ref[pl.ds(g * each, each)] = joined.reshape(each, half, 128)


def attend(qkv, seg):
    blocks, _, half, _ = qkv.shape
    total = blocks * half * 2
    steps = total // (2 * ROWS)
    return pl.pallas_call(
        attend_kernel,
        grid=(steps,),
        in_specs=[whole(qkv.shape), whole((total, 1)), whole((1, total))],
        out_specs=[whole((blocks, half, 128)), whole((HD, total)), whole((1, total))],
        out_shape=[
            jax.ShapeDtypeStruct((blocks, half, 128), BF),
            jax.ShapeDtypeStruct((HD, total), F32),
            jax.ShapeDtypeStruct((1, total), F32),
        ],
        scratch_shapes=[
            pltpu.VMEM((total, HD), BF),
            pltpu.VMEM((total, HD), BF),
            pltpu.VMEM((total, HD), BF),
            pltpu.VMEM((HD, total), BF),
        ],
        compiler_params=pltpu.CompilerParams(vmem_limit_bytes=VMEM),
        name="attend",
    )(qkv, seg[:, None], seg[None, :])


def attend_back_kernel(
    qkv_ref, do_ref, attn_ref, lse_ref, segc_ref, segr_ref, cos_ref, sin_ref,
    out_ref, flat_ref,
    q_s, k_s, v_s, do_s, delta_s, dq_s,
):
    g = pl.program_id(0)
    steps = pl.num_programs(0)
    half = qkv_ref.shape[-2]
    each = ROWS // half
    scale = 1.0 / math.sqrt(HD)

    @pl.when(g == 0)
    def _():
        total = q_s.shape[0] // (2 * ROWS)
        unpack_all(qkv_ref, 0, q_s, total)
        unpack_all(qkv_ref, 1, k_s, total)
        unpack_all(qkv_ref, 2, v_s, total)
        unpack_all(do_ref, 0, do_s, total)
        do_t = jnp.transpose(do_s[...].astype(F32))
        delta_s[...] = jnp.sum(do_t * attn_ref[...], 0, keepdims=True)
        dq_s[...] = jnp.zeros_like(dq_s)

    at = pl.multiple_of(g * 2 * ROWS, 2 * ROWS)
    here = pl.ds(at, 2 * ROWS)
    keys = k_s[here]
    scores = mm_nt(keys, q_s[...])
    allowed = segc_ref[here] == segr_ref[...]
    probs = jnp.where(allowed, jnp.exp(scores - lse_ref[...]), 0.0)
    prob_grad = mm_nt(v_s[here], do_s[...])
    score_grad = (probs * (prob_grad - delta_s[...])).astype(BF)
    value_grad = mm(probs.astype(BF), do_s[...])
    key_grad = mm(score_grad, q_s[...])
    keys_t = jnp.transpose(keys.astype(F32)).astype(BF)
    dq_s[...] += mm(keys_t, score_grad)

    def unrotate(rows, where):
        swapped = jnp.concatenate([rows[:, HD // 2 :], rows[:, : HD // 2]], 1)
        return rows * cos_ref[where] + swapped * sin_ref[where]

    def put(part, step, rows):
        low = rows.astype(BF)
        flat_ref[part * HD : (part + 1) * HD, pl.ds(pl.multiple_of(step * 2 * ROWS, 2 * ROWS), 2 * ROWS)] = (
            jnp.transpose(rows).astype(BF)
        )
        joined = jnp.concatenate([low[:ROWS].astype(F32), low[ROWS:].astype(F32)], 1).astype(BF)
        out_ref[pl.ds(step * each, each), part] = joined.reshape(each, half, 128)

    put(1, g, unrotate(key_grad, here))
    put(2, g, value_grad)

    @pl.when(g == steps - 1)
    def _():
        for s in range(q_s.shape[0] // (2 * ROWS)):
            there = slice(s * 2 * ROWS, (s + 1) * 2 * ROWS)
            rows = jnp.transpose(dq_s[:, there]) * scale
            put(0, s, unrotate(rows, there))


def attend_back(qkv, attn_grad, attn_t, lse, seg, cos_rows, sin_rows):
    blocks, _, half, _ = qkv.shape
    total = blocks * half * 2
    steps = total // (2 * ROWS)
    return pl.pallas_call(
        attend_back_kernel,
        grid=(steps,),
        in_specs=[
            whole(qkv.shape), whole((blocks, 1, half, 128)), whole((HD, total)), whole((1, total)),
            whole((total, 1)), whole((1, total)), whole((total, HD)), whole((total, HD)),
        ],
        out_specs=[whole((blocks, 3, half, 128)), whole((3 * HD, total))],
        out_shape=[
            jax.ShapeDtypeStruct((blocks, 3, half, 128), BF),
            jax.ShapeDtypeStruct((3 * HD, total), BF),
        ],
        scratch_shapes=[
            pltpu.VMEM((total, HD), BF),
            pltpu.VMEM((total, HD), BF),
            pltpu.VMEM((total, HD), BF),
            pltpu.VMEM((total, HD), BF),
            pltpu.VMEM((1, total), F32),
            pltpu.VMEM((HD, total), F32),
        ],
        compiler_params=pltpu.CompilerParams(vmem_limit_bytes=VMEM),
        name="attend_back",
    )(qkv, attn_grad[:, None], attn_t, lse, seg[:, None], seg[None, :], cos_rows, sin_rows)


def local(
    frames, skip_input, lengths, w_skip, b_skip, g_attn, w_qkv, w_out, g_ff, w_up, b_up, w_down, b_down, out_grad
):
    tok, width = frames.shape
    blocks = lax.axis_size("blk")
    packs = lax.axis_size("pack")
    me = lax.axis_index("blk")
    mine = lax.axis_index("pack") % 2
    rows = width // blocks
    repeat = blocks // H
    half = tok // 2
    planes = 4
    plane = blocks // planes
    spot = me % plane
    place = me // plane
    plane_groups = [[z * plane + j for j in range(plane)] for z in range(planes)]
    column_groups = [[z * plane + j for z in range(planes)] for j in range(plane)]
    swap = [(i, i ^ 1) for i in range(packs)]

    def to_peer(block):
        return lax.ppermute(block, "pack", swap)

    def over_pairs(block):
        total = block
        for k in range(1, packs // 2):
            total = total + lax.ppermute(block, "pack", [(i, (i + 2 * k) % packs) for i in range(packs)])
        return total

    def all_to_all(block, groups=None):
        return lax.all_to_all(block, "blk", 0, 0, tiled=True, axis_index_groups=groups)

    vectors = jnp.stack([b_skip, g_attn, g_ff, b_down] + list(b_up.reshape(4, rows)), 0)
    vectors = jnp.transpose(jnp.pad(vectors, ((0, 120), (0, 0))))
    first_part = jnp.concatenate([w_skip[:rows], w_skip[rows:], w_qkv, vectors], 1)
    gathered = lax.all_gather(first_part, "blk", axis=0, tiled=True)
    up_cols = jnp.transpose(w_up.reshape(rows, blocks, 4, rows), (0, 2, 1, 3)).reshape(rows, 2, 2 * width)
    up_mine = lax.dynamic_index_in_dim(up_cols, mine, 1, keepdims=False)
    down_mine = lax.dynamic_slice_in_dim(w_down, mine * 2 * rows, 2 * rows, 0)
    second_part = jnp.concatenate([w_out, up_mine, down_mine[:rows], down_mine[rows:]], 1)
    gathered, second_part = lax.optimization_barrier((gathered, second_part))
    gathered_more = lax.all_gather(second_part, "blk", axis=0, tiled=True)
    skip_a, skip_b = gathered[:, :width], gathered[:, width : 2 * width]
    qkv_full = gathered[:, 2 * width : 5 * width]
    small = jnp.transpose(gathered[:, 5 * width :].astype(F32))[:8]
    bias_skip, gain_attn, gain_ff, bias_down = small[0], small[1], small[2], small[3]
    bias_up = lax.dynamic_slice_in_dim(small, 4 + 2 * mine, 2, 0).reshape(2 * width)

    pack_lengths = lengths[0]
    _, offset = segment_of(me * tok + jnp.arange(tok, dtype=jnp.int32), pack_lengths)
    cosine, sine = angles(offset)
    cos_pair = jnp.concatenate([cosine] * 4, 1)
    sin_pair = jnp.concatenate([-sine, sine, -sine, sine], 1)
    index = jnp.arange(tok * blocks, dtype=jnp.int32)
    packed_row = (index // (2 * ROWS)) * ROWS + index % ROWS
    lane_half = (index // ROWS) % 2
    token = (packed_row // half) * tok + lane_half * half + packed_row % half
    seg_all, offset_all = segment_of(token, pack_lengths)
    cos_all, sin_all = angles(offset_all)
    cos_rows = jnp.concatenate([cos_all, cos_all], 1)
    sin_rows = jnp.concatenate([sin_all, -sin_all], 1)

    joined = jnp.concatenate([frames, skip_input], 1)
    joined_split = joined.reshape(tok, planes, plane, 2 * rows)
    joined_share = all_to_all(
        jnp.transpose(joined_split, (2, 0, 1, 3)).reshape(plane, tok, planes * 2 * rows), plane_groups
    )
    grad_peer = to_peer(out_grad)
    out_grad_two = jnp.concatenate([out_grad, grad_peer], 0)

    by_piece = joined.reshape(tok, blocks, 2, rows)
    joined_a = by_piece[:, :, 0].reshape(tok, width)
    joined_b = by_piece[:, :, 1].reshape(tok, width)
    stream_in = mm(joined_a, skip_a) + mm(joined_b, skip_b) + bias_skip
    root_in = lax.rsqrt(jnp.mean(stream_in * stream_in, -1, keepdims=True) + EPSILON)
    unit_in = stream_in * root_in
    normed_attn = (unit_in * gain_attn).astype(BF)
    projected = mm(normed_attn, qkv_full)
    qkv_packed = rope_pack(projected, cos_pair, sin_pair)
    if repeat > 1:
        qkv_packed = jnp.repeat(qkv_packed, repeat, 0)
    qkv_head = all_to_all(qkv_packed)
    attn_packed, attn_t, lse = attend(qkv_head, seg_all)
    attn_back = all_to_all(attn_packed)[::repeat]
    attn_low = unpack_heads(attn_back[:, None])
    out_full = gathered_more[:, :width]
    up_half = gathered_more[:, width : 3 * width]
    down_a, down_b = gathered_more[:, 3 * width : 4 * width], gathered_more[:, 4 * width :]
    stream_mid = stream_in + mm(attn_low, out_full)
    root_mid = lax.rsqrt(jnp.mean(stream_mid * stream_mid, -1, keepdims=True) + EPSILON)
    unit_mid = stream_mid * root_mid
    normed_ff = (unit_mid * gain_ff).astype(BF)
    normed_two = jnp.concatenate([normed_ff, to_peer(normed_ff)], 0)
    hidden_pre = mm(normed_two, up_half) + bias_up
    act_grad = jnp.concatenate([mm_nt(out_grad_two, down_a), mm_nt(out_grad_two, down_b)], 1)
    hidden, gelu_back = jax.vjp(activation, hidden_pre)
    hidden_act = hidden.astype(BF)
    pre_grad = gelu_back(act_grad)[0].astype(BF)
    ff_grad_two = mm_nt(pre_grad, up_half)
    ff_grad = ff_grad_two[:tok] + to_peer(ff_grad_two[tok:].astype(BF)).astype(F32)
    ff_two = mm(hidden_act[:, :width], down_a) + mm(hidden_act[:, width:], down_b)
    layer_out = (
        stream_mid + (ff_two[:tok] + to_peer(ff_two[tok:].astype(BF)).astype(F32)) + bias_down
    ).astype(BF)

    scaled = ff_grad * gain_ff
    grad_gff = jnp.sum(ff_grad * unit_mid, 0)
    mid_grad = out_grad.astype(F32) + root_mid * (scaled - unit_mid * jnp.mean(scaled * unit_mid, -1, keepdims=True))
    branch_grad = mid_grad.astype(BF)
    attn_grad = pack_heads(mm_nt(branch_grad, out_full).astype(BF))
    if repeat > 1:
        attn_grad = jnp.repeat(attn_grad, repeat, 0)
    attn_grad_head = all_to_all(attn_grad)

    grad_up = mm_tn(normed_two, pre_grad)
    grad_down_a = mm_tn(hidden_act[:, :width], out_grad_two)
    grad_down_b = mm_tn(hidden_act[:, width:], out_grad_two)
    grad_out = mm_tn(attn_low, branch_grad)
    vec = jnp.concatenate(
        [
            grad_gff[None],
            jnp.sum(out_grad.astype(F32), 0)[None],
            jnp.sum(pre_grad.astype(F32), 0).reshape(2, width),
        ],
        0,
    )
    vec = jnp.transpose(jnp.pad(vec, ((0, 124), (0, 0)))).astype(BF)
    shares = lax.psum_scatter(
        jnp.concatenate(
            [grad_up.astype(BF), grad_down_a.astype(BF), grad_down_b.astype(BF), grad_out.astype(BF), vec], 1
        ),
        "blk",
        scatter_dimension=0,
        tiled=True,
    )
    if packs > 2:
        shares = over_pairs(shares.astype(F32)).astype(BF)
    others = to_peer(shares).astype(F32)
    shares = shares.astype(F32)

    def both(own, other):
        return jnp.where(mine == 0, jnp.stack([own, other]), jnp.stack([other, own]))

    up_pair = both(shares[:, : 2 * width], others[:, : 2 * width])
    up_pair = jnp.transpose(up_pair, (1, 0, 2)).reshape(rows, 4, blocks, rows)
    w_up_grad = jnp.transpose(up_pair, (0, 2, 1, 3)).reshape(rows, 4 * width)
    down_pair = both(shares[:, 2 * width : 4 * width], others[:, 2 * width : 4 * width])
    w_down_grad = jnp.transpose(down_pair.reshape(2, rows, 2, width), (0, 2, 1, 3)).reshape(4 * rows, width)
    w_out_grad = shares[:, 4 * width : 5 * width] + others[:, 4 * width : 5 * width]
    vec_own, vec_other = jnp.transpose(shares[:, 5 * width :]), jnp.transpose(others[:, 5 * width :])
    g_ff_grad = vec_own[0] + vec_other[0]
    b_down_grad = vec_own[1] + vec_other[1]
    b_up_grad = both(vec_own[2:4], vec_other[2:4]).reshape(4 * rows)

    normed_full = lax.all_gather(normed_attn, "blk", axis=0, tiled=True)
    dqkv_packed, dqkv_t = attend_back(qkv_head, attn_grad_head, attn_t, lse, seg_all, cos_rows, sin_rows)
    dqkv_back = all_to_all(dqkv_packed)[::repeat]
    projected_grad = unpack_heads(dqkv_back)
    normed_grad = mm_nt(projected_grad, qkv_full)
    scaled_in = normed_grad * gain_attn
    grad_gattn = jnp.sum(normed_grad * unit_in, 0)
    in_grad = mid_grad + root_in * (scaled_in - unit_in * jnp.mean(scaled_in * unit_in, -1, keepdims=True))
    in_low = in_grad.astype(BF)
    joined_grad_a = mm_nt(in_low, skip_a).astype(BF).reshape(tok, blocks, 1, rows)
    joined_grad_b = mm_nt(in_low, skip_b).astype(BF).reshape(tok, blocks, 1, rows)
    joined_grad = jnp.concatenate([joined_grad_a, joined_grad_b], 2).reshape(tok, 2 * width)
    frames_grad = joined_grad[:, :width]
    skip_grad = joined_grad[:, width:]

    normed_order = normed_full.reshape(blocks * half // ROWS, ROWS // half, 2, half, width)
    normed_order = jnp.transpose(normed_order, (0, 2, 1, 3, 4)).reshape(blocks * tok, width)
    qkv_grad_t = mm(dqkv_t, normed_order).astype(BF)
    side = 128 // rows
    folded = qkv_grad_t.reshape(side, 3 * HD // side, blocks, rows)
    folded = jnp.transpose(folded, (2, 1, 0, 3)).reshape(blocks, 3 * HD // side, 128)
    folded = all_to_all(folded)[::repeat]
    qkv_share = jnp.transpose(folded.reshape(H, 3 * HD // side, side, rows), (3, 2, 1, 0))
    qkv_share = qkv_share.reshape(rows, 3, HD, H)
    qkv_share = jnp.transpose(qkv_share, (0, 1, 3, 2)).reshape(rows, 3 * width)
    if packs > 2:
        qkv_share = over_pairs(qkv_share.astype(F32)).astype(BF)
    w_qkv_grad = qkv_share.astype(F32) + to_peer(qkv_share).astype(F32)

    extra = jnp.pad(grad_gattn[None].astype(BF), ((0, 15), (0, 0)))
    tail = jnp.concatenate([in_low, extra], 0)
    inner = plane // 2
    pieces = [tail]
    for k in range(1, inner):
        route = [
            (i, (i // plane) * plane + ((i % plane) // 2 + k) % inner * 2 + i % 2) for i in range(blocks)
        ]
        pieces.append(lax.ppermute(tail, "blk", route))
    column = jnp.stack(pieces)
    across = lax.ppermute(column, "blk", [(i, i ^ 1) for i in range(blocks)])
    tails = jnp.concatenate([column, across], 0)
    step = jnp.arange(inner, dtype=jnp.int32)
    from_spot = jnp.concatenate(
        [((spot // 2 - step) % inner) * 2 + spot % 2, ((spot // 2 - step) % inner) * 2 + 1 - spot % 2]
    )
    joined_in_order = jnp.concatenate(
        [lax.dynamic_index_in_dim(joined_share, from_spot[j], 0, keepdims=False) for j in range(plane)], 0
    )
    low_all = tails[:, :tok].reshape(plane * tok, width)
    skip_part = mm_tn(joined_in_order, low_all).astype(BF).reshape(planes, 2 * rows, width)
    vec_tail = jnp.stack(
        [jnp.sum(low_all.astype(F32), 0), jnp.sum(tails[:, tok].astype(F32), 0)] + [jnp.zeros((width,), F32)] * 14
    ).astype(BF)
    payload = jnp.concatenate([skip_part, jnp.broadcast_to(vec_tail[None], (planes, 16, width))], 1)
    arrived = all_to_all(payload, column_groups)
    summed = jnp.sum(arrived.astype(F32), 0)
    if packs > 2:
        summed = over_pairs(summed)
    total = summed + to_peer(summed.astype(BF)).astype(F32)
    w_skip_grad = total[: 2 * rows]
    own = lax.dynamic_slice_in_dim(total[2 * rows : 2 * rows + 2], me * rows, rows, 1)
    return (
        layer_out, frames_grad, skip_grad, w_skip_grad, own[0], own[1], w_qkv_grad, w_out_grad, g_ff_grad,
        w_up_grad, b_up_grad, w_down_grad, b_down_grad,
    )


def solution(mesh):
    token_spec = P(("pack", "blk"), None)
    matrix, vector = P("blk", None), P("blk")
    return jax.shard_map(
        local,
        mesh=mesh,
        in_specs=(
            token_spec, token_spec, P("pack", None), matrix, vector, vector, matrix, matrix, vector, matrix, vector,
            matrix, vector, token_spec,
        ),
        out_specs=(
            token_spec, token_spec, token_spec, matrix, vector, vector, matrix, matrix, vector, matrix, vector, matrix,
            vector,
        ),
        check_vma=False,
    )
```

time: 1310 us -> 502 us (0.38)
  waiting for transfers between devices: 884 us -> 213 us
  matrix products: 175 us -> 61.3 us
  blocking collectives: 121 us -> 41.9 us
  starting transfers between devices: 1.53 us -> 48.5 us
  Pallas kernels: 0 us -> 44 us
  other arithmetic: 56 us -> 22.7 us
    reduce_scatter x5 -> x1, waiting for transfers between devices: 356 us -> 0.01 us  [local(): lax.psum_scatter(jnp.concatenate([grad_up.astype(BF), grad_down_a.astype(...]
    ppermute x32 -> x9, waiting for transfers between devices: 228 us -> 32.6 us  [the longest x7 27.8 us: to_peer(): return lax.ppermute(block, 'pack', swap)]
    all_gather x7 -> x3, waiting for transfers between devices: 297 us -> 107 us  [the longest x1 88.4 us: local(): gathered = lax.all_gather(first_part, 'blk', axis=0, tiled=True)]
    dot_general x97 -> x20, matrix products: 175 us -> 61.3 us  [the longest x7 30 us: mm_nt(): lax.dot_general(left, right, (((1,), (1,)), ((), ())), preferred_element_...]
    unnamed x2 -> x0, blocking collectives: 96.4 us -> none
    all_to_all x0 -> x6, waiting for transfers between devices: none -> 72.1 us  [all_to_all(): lax.all_to_all(block, 'blk', 0, 0, tiled=True, axis_index_groups=groups)]
    pallas_call x0 -> x6, Pallas kernels: none -> 44 us  [the longest x1 20.2 us: attend_back(): pl.pallas_call(attend_back_kernel, grid=(steps,), in_specs=[whole(qkv.sha...]
    all_to_all x0 -> x1, blocking collectives: none -> 41.9 us  [all_to_all(): lax.all_to_all(block, 'blk', 0, 0, tiled=True, axis_index_groups=groups)]
  transfers between devices with their start and end apart: 45 -> 19, of which waited for: 43 -> 13; matrix products, arithmetic and copies ran while one was open for 19% -> 21% of each run, Pallas kernels for 0% -> 9%
where the time goes in v1:
time: 502 us; the launch traced here: 494 us
  waiting for transfers between devices  213 us (42%)
  matrix products  61.3 us (12%)
  starting transfers between devices  48.5 us (10%)
  Pallas kernels  44 us (9%)
  blocking collectives  41.9 us (8%)
  local copies, waits for them, and re-layouts  39.7 us (8%)
  between operations  22.8 us (5%)
  other arithmetic  22.7 us (5%)
    all_gather x1, waiting for transfers between devices, local(): gathered = lax.all_gather(first_part, 'blk', axis=0, tiled=True)  88.4 us
    all_to_all x6, waiting for transfers between devices, all_to_all(): lax.all_to_all(block, 'blk', 0, 0, tiled=True, axis_index_groups=groups)  72.1 us
    all_to_all x1, blocking collectives, all_to_all(): lax.all_to_all(block, 'blk', 0, 0, tiled=True, axis_index_groups=groups)  41.9 us
    all_to_all x6, starting transfers between devices, all_to_all(): lax.all_to_all(block, 'blk', 0, 0, tiled=True, axis_index_groups=groups)  34.7 us
    dot_general x7, matrix products, mm_nt(): lax.dot_general(left, right, (((1,), (1,)), ((), ())), preferred_element_...  30 us
    ppermute x7, waiting for transfers between devices, to_peer(): return lax.ppermute(block, 'pack', swap)  27.8 us
    pallas_call x1, Pallas kernels, attend_back(): pl.pallas_call(attend_back_kernel, grid=(steps,), in_specs=[whole(qkv.sha...  20.2 us
    all_gather x1, waiting for transfers between devices, local(): gathered_more = lax.all_gather(second_part, 'blk', axis=0, tiled=True)  18.7 us
  transfers between devices with their start and end apart: 19, of which 13 were waited for; matrix products, arithmetic and copies ran while one was open for 21% of the time, Pallas kernels for 9%

profile of v1, /device:TPU:0, one launch (start us, length us, event | category | flops | bytes accessed | tf_op | source)
XLA Modules:
  0.0 493.5 jit_solution(1112225666659264687)
XLA Ops:
  15.8 88.4 %all-gather.4.cloned.1.call-done = bf16[1024,5248]{1,0:T(8,128)(2,1)} async-done(((bf16[64,5248]{1,0:T(8,128)(2,1)}), bf16[1024,5248]{1,0:T(8,128)(2,1)}) %all-gather.4.cloned.1.call-update) | async-done | bytes 10747920 | tf_op jit(solution)/shard_map/all_gather | solution.py:320
  112.5 5.4 %fusion.2.proj_ref = f32[128,3072]{1,0:T(8,128)} fusion(bf16[128,1024]{1,0:T(8,128)(2,1)S(1)} %multiply_convert_fusion.2, bf16[1024,5248]{1,0:T(8,128)(2,1)} %all-gather.4.cloned.1.call-done), kind=kOutput, calls=%fused_computation.2 | convolution fusion | flops 805306368 | bytes 8126464 | tf_op jit(solution)/shard_map/dot_general | solution.py:22
  118.0 4.2 rope_pack.1
  129.7 23.4 %all-to-all-done.qkv_ref = bf16[16,3,64,128]{3,2,1,0:T(8,128)(2,1)S(1)} async-done(((bf16[16,3,64,128]{3,2,1,0:T(8,128)(2,1)}), bf16[16,3,64,128]{3,2,1,0:T(8,128)(2,1)S(1)}, u32[]{:S(2)}, u32[]{:S(2)}) %all-to-all-start) | async-done | bytes 786464 | tf_op jit(solution)/shard_map/all_to_all | solution.py:315
  153.9 13.7 %attend.1 = (bf16[16,64,128]{2,1,0:T(8,128)(2,1)}, f32[64,2048]{1,0:T(8,128)}, f32[1,2048]{1,0:T(1,128)}) custom-call(bf16[16,3,64,128]{3,2,1,0:T(8,128)(2,1)} %copy-done, s32[2048,1]{1,0:T(8,128)} %copy.154.segc_ref, s32[1,2048]{1,0:T(1,128)} %bitcast.144), custom_call_target="tpu_custom_call" | custom-call | tf_op jit(solution)/shard_map/attend/pallas_call | solution.py:178
  167.6 5.6 %all-to-all-start.1 = ((bf16[16,64,128]{2,1,0:T(8,128)(2,1)}), bf16[16,64,128]{2,1,0:T(8,128)(2,1)S(1)}, u32[]{:S(2)}, u32[]{:S(2)}) async-start(bf16[16,64,128]{2,1,0:T(8,128)(2,1)} %get-tuple-element.21), calls=%async_computation.1 | async-start | bytes 524288 | tf_op jit(solution)/shard_map/all_to_all | solution.py:315
  174.1 13.8 %all-to-all-done.1 = bf16[16,64,128]{2,1,0:T(8,128)(2,1)S(1)} async-done(((bf16[16,64,128]{2,1,0:T(8,128)(2,1)}), bf16[16,64,128]{2,1,0:T(8,128)(2,1)S(1)}, u32[]{:S(2)}, u32[]{:S(2)}) %all-to-all-start.1) | async-done | bytes 262176 | tf_op jit(solution)/shard_map/all_to_all | solution.py:315
  190.4 18.7 %all-gather.6.cloned.1.call-done = bf16[1024,5120]{1,0:T(8,128)(2,1)} async-done(((bf16[64,5120]{1,0:T(8,128)(2,1)}), bf16[1024,5120]{1,0:T(8,128)(2,1)}) %all-gather.6.cloned.1.call-update) | async-done | bytes 10485776 | tf_op jit(solution)/shard_map/all_gather | solution.py:326
  230.1 4.8 convert_dynamic-update-slice_fusion
  247.2 13.7 %fusion.56.in_ref = bf16[128,1024]{1,0:T(8,128)(2,1)} fusion(bf16[1024,5120]{1,0:T(8,128)(2,1)} %all-gather.6.cloned.1.call-done, f32[128,1024]{1,0:T(8,128)S(1)} %get-tuple-element.114), kind=kOutput, calls=%fused_computation.55 | convolution fusion | flops 268697600 | bytes 2883584 | tf_op jit(solution)/shard_map/dot_general | solution.py:26
  262.7 3.8 all-to-all-start.2
  266.6 3.7 multiply_sine_fusion
  272.2 4.4 all-to-all-done.2
  277.3 20.2 %attend_back.1 = (bf16[16,3,64,128]{3,2,1,0:T(8,128)(2,1)}, bf16[192,2048]{1,0:T(8,128)(2,1)}) custom-call(bf16[16,3,64,128]{3,2,1,0:T(8,128)(2,1)} %copy-done, bf16[16,1,64,128]{3,2,1,0:T(8,128)(2,1)} %bitcast.135, f32[64,2048]{1,0:T(8,128)} %get-tuple-element.23.attn_ref, f32[1,2048]{1,0:T(1,128)} %get-tuple-element.24.lse_ref, s32[2048,1]{1,0:T(8,128)} %copy.154.segc_ref, ...), custom_call_target="tpu_custom_call" | custom-call | tf_op jit(solution)/shard_map/attend_back/pallas_call | solution.py:261
  297.5 41.9 %all_to_all.35.in_ref = bf16[16,3,64,128]{3,2,1,0:T(8,128)(2,1)} all-to-all(bf16[16,3,64,128]{3,2,1,0:T(8,128)(2,1)} %get-tuple-element.25), channel_id=1, replica_groups=mesh['pack'=2,'blk'=16] {'blk'}, dimensions={0} | all-to-all | bytes 1572864 | tf_op jit(solution)/shard_map/all_to_all | solution.py:315
  341.8 5.5 %multiply_reduce_fusion.1 = (bf16[1024]{0:T(1024)(128)(2,1)S(1)}, f32[128]{0:T(128)S(1)}, f32[128,1024]{1,0:T(8,128)S(1)}) fusion(f32[128,1024]{1,0:T(8,128)S(1)} %get-tuple-element.143, f32[128]{0:T(128)S(1)} %add_rsqrt_fusion.1, f32[1024]{0:T(1024)S(1)} %get-tuple-element.98, bf16[128,3072]{1,0:T(8,128)(2,1)} %unpack_heads.3, ...), kind=kOutput, calls=%fused_computation.97 | convolution fusion | flops 806091648 | bytes 8133632 | tf_op jit(solution)/shard_map/dot_general | solution.py:26
  356.7 4.8 collective-permute-done.4
  377.5 10.1 %all-to-all-start.6 = ((bf16[16,96,128]{2,1,0:T(8,128)(2,1)}), bf16[16,96,128]{2,1,0:T(8,128)(2,1)S(1)}, u32[]{:S(2)}, u32[]{:S(2)}) async-start(bf16[16,96,128]{2,1,0:T(8,128)(2,1)} %copy.165), calls=%async_computation.6 | async-start | bytes 786432 | tf_op jit(solution)/shard_map/all_to_all | solution.py:315
  392.1 12.0 %all-to-all-done.6 = bf16[16,96,128]{2,1,0:T(8,128)(2,1)S(1)} async-done(((bf16[16,96,128]{2,1,0:T(8,128)(2,1)}), bf16[16,96,128]{2,1,0:T(8,128)(2,1)S(1)}, u32[]{:S(2)}, u32[]{:S(2)}) %all-to-all-start.6) | async-done | bytes 393248 | tf_op jit(solution)/shard_map/all_to_all | solution.py:315
  404.2 8.1 %all-to-all-start.5 = ((bf16[4,144,1024]{2,1,0:T(8,128)(2,1)}), bf16[4,144,1024]{2,1,0:T(8,128)(2,1)S(1)}, u32[]{:S(2)}, u32[]{:S(2)}) async-start(bf16[4,144,1024]{2,1,0:T(8,128)(2,1)} %pad_maximum_fusion.2), calls=%async_computation.5 | async-start | bytes 2359296 | tf_op jit(solution)/shard_map/all_to_all | solution.py:315
  416.6 8.3 %collective-permute-done.7 = bf16[64,3072]{1,0:T(8,128)(2,1)S(1)} collective-permute-done((bf16[64,3072]{1,0:T(8,128)(2,1)S(1)}, bf16[64,3072]{1,0:T(8,128)(2,1)S(1)}, u32[]{:S(2)}, u32[]{:S(2)}) %collective-permute-start.7) | collective-permute-done | bytes 393248 | tf_op jit(solution)/shard_map/ppermute | solution.py:306
  431.1 15.8 %all-to-all-done.5 = bf16[4,144,1024]{2,1,0:T(8,128)(2,1)S(1)} async-done(((bf16[4,144,1024]{2,1,0:T(8,128)(2,1)}), bf16[4,144,1024]{2,1,0:T(8,128)(2,1)S(1)}, u32[]{:S(2)}, u32[]{:S(2)}) %all-to-all-start.5) | async-done | bytes 1179680 | tf_op jit(solution)/shard_map/all_to_all | solution.py:315
  450.7 5.3 %collective-permute-done.6 = bf16[144,1024]{1,0:T(8,128)(2,1)S(1)} collective-permute-done((bf16[144,1024]{1,0:T(8,128)(2,1)S(1)}, bf16[144,1024]{1,0:T(8,128)(2,1)S(1)}, u32[]{:S(2)}, u32[]{:S(2)}) %collective-permute-start.6) | collective-permute-done | bytes 294944 | tf_op jit(solution)/shard_map/ppermute | solution.py:306
  461.9 11.9 %collective-permute-done.8 = bf16[64,5248]{1,0:T(8,128)(2,1)S(1)} collective-permute-done((bf16[64,5248]{1,0:T(8,128)(2,1)}, bf16[64,5248]{1,0:T(8,128)(2,1)S(1)}, u32[]{:S(2)}, u32[]{:S(2)}) %collective-permute-start.8) | collective-permute-done | bytes 671776 | tf_op jit(solution)/shard_map/ppermute | solution.py:306
  (228 shorter events, 123.1 us)
Async XLA Ops:
  7.2 97.0 %all-gather.4.cloned.1.call-start = ((), (), s32[]{:S(2)}) async-start(), calls=%async_computation.8 | async-start | bytes 11419648 | tf_op jit(solution)/shard_map/all_gather | solution.py:320
  11.9 197.2 %all-gather.6.cloned.1.call-start = ((), (), s32[]{:S(2)}) async-start(), calls=%async_computation.9 | async-start | bytes 11141120 | tf_op jit(solution)/shard_map/all_gather | solution.py:326
  14.1 90.1 %copy-start.18 = (bf16[128,1024]{1,0:T(8,128)(2,1)S(1)}, bf16[128,1024]{1,0:T(8,128)(2,1)}, u32[]{:S(2)}) copy-start(bf16[128,1024]{1,0:T(8,128)(2,1)} %param.15) | copy-start | bytes 786436
  14.7 89.7 %copy-start.19 = (bf16[128,1024]{1,0:T(8,128)(2,1)S(1)}, bf16[128,1024]{1,0:T(8,128)(2,1)}, u32[]{:S(2)}) copy-start(bf16[128,1024]{1,0:T(8,128)(2,1)} %param.14) | copy-start | bytes 786436
  14.7 89.9 %copy-start.26 = (s32[1,4]{1,0:T(1,128)S(1)}, s32[1,4]{1,0:T(1,128)}, u32[]{:S(2)}) copy-start(s32[1,4]{1,0:T(1,128)} %param.16) | copy-start | bytes 52
  122.2 30.9 %all-to-all-start = ((bf16[16,3,64,128]{3,2,1,0:T(8,128)(2,1)}), bf16[16,3,64,128]{3,2,1,0:T(8,128)(2,1)S(1)}, u32[]{:S(2)}, u32[]{:S(2)}) async-start(bf16[16,3,64,128]{3,2,1,0:T(8,128)(2,1)} %rope_pack.1), calls=%async_computation | async-start | bytes 1572864 | tf_op jit(solution)/shard_map/all_to_all | solution.py:315
  125.8 246.4 %all-gather.8.cloned.1.call-start = ((), (), s32[]{:S(2)}) async-start(), calls=%async_computation.10 | async-start | bytes 4456448 | tf_op jit(solution)/shard_map/all_gather | solution.py:439
  126.5 47.1 %collective-permute-start.2 = (bf16[128,1024]{1,0:T(8,128)(2,1)S(1)}, bf16[128,1024]{1,0:T(8,128)(2,1)S(1)}, u32[]{:S(2)}, u32[]{:S(2)}) collective-permute-start(bf16[128,1024]{1,0:T(8,128)(2,1)S(1)} %copy-done.9), channel_id=1, source_target_pairs={{0,16},{16,0},{1,17},{17,1},{2,18},{18,2},{3,19},{19,3},{4,20},{20... | collective-permute-start | bytes 786440 | tf_op jit(solution)/shard_map/ppermute | solution.py:306
  128.3 24.8 %copy-start.21 = (s32[2048]{0:T(1024)}, s32[2048]{0:T(1024)S(1)}, u32[]{:S(2)}) copy-start(s32[2048]{0:T(1024)S(1)} %get-tuple-element.103) | copy-start | bytes 24580
  167.6 20.2 %all-to-all-start.1 = ((bf16[16,64,128]{2,1,0:T(8,128)(2,1)}), bf16[16,64,128]{2,1,0:T(8,128)(2,1)S(1)}, u32[]{:S(2)}, u32[]{:S(2)}) async-start(bf16[16,64,128]{2,1,0:T(8,128)(2,1)} %get-tuple-element.21), calls=%async_computation.1 | async-start | bytes 524288 | tf_op jit(solution)/shard_map/all_to_all | solution.py:315
  173.2 284.3 %reduce-scatter.2.cloned.1.call-start = ((), (), s32[]{:S(2)}) async-start(), calls=%async_computation.11 | async-start | bytes 11419648 | tf_op jit(solution)/shard_map/reduce_scatter | solution.py:412
  173.7 41.8 %copy-start.24 = (bf16[256,1024]{1,0:T(8,128)(2,1)}, bf16[256,1024]{1,0:T(8,128)(2,1)S(1)}, u32[]{:S(2)}) copy-start(bf16[256,1024]{1,0:T(8,128)(2,1)S(1)} %constant_dynamic-update-slice_fusion) | copy-start | bytes 1572868
  211.6 8.5 %collective-permute-start = (bf16[128,1024]{1,0:T(8,128)(2,1)S(1)}, bf16[128,1024]{1,0:T(8,128)(2,1)S(1)}, u32[]{:S(2)}, u32[]{:S(2)}) collective-permute-start(bf16[128,1024]{1,0:T(8,128)(2,1)S(1)} %multiply_convert_fusion.1), channel_id=1, source_target_pairs={{0,16},{16,0},{1,17},{17,1},{2,18},{18,2},{3,19},{19,3},{4,20},{20... | collective-permute-start | bytes 786440 | tf_op jit(solution)/shard_map/ppermute | solution.py:306
  225.0 14.3 %collective-permute-start.3 = (bf16[128,1024]{1,0:T(8,128)(2,1)}, bf16[128,1024]{1,0:T(8,128)(2,1)S(1)}, u32[]{:S(2)}, u32[]{:S(2)}) collective-permute-start(bf16[128,1024]{1,0:T(8,128)(2,1)} %slice.342), channel_id=1, source_target_pairs={{0,16},{16,0},{1,17},{17,1},{2,18},{18,2},{3,19},{19,3},{4,20},{20... | collective-permute-start | bytes 786440 | tf_op jit(solution)/shard_map/ppermute | solution.py:306
  229.5 10.9 %collective-permute-start.1 = (bf16[128,1024]{1,0:T(8,128)(2,1)}, bf16[128,1024]{1,0:T(8,128)(2,1)S(1)}, u32[]{:S(2)}, u32[]{:S(2)}) collective-permute-start(bf16[128,1024]{1,0:T(8,128)(2,1)} %slice.343), channel_id=1, source_target_pairs={{0,16},{16,0},{1,17},{17,1},{2,18},{18,2},{3,19},{19,3},{4,20},{20... | collective-permute-start | bytes 786440 | tf_op jit(solution)/shard_map/ppermute | solution.py:306
  262.7 13.9 %all-to-all-start.2 = ((bf16[16,64,128]{2,1,0:T(8,128)(2,1)}), bf16[16,64,128]{2,1,0:T(8,128)(2,1)S(1)}, u32[]{:S(2)}, u32[]{:S(2)}) async-start(bf16[16,64,128]{2,1,0:T(8,128)(2,1)} %pack_heads.1), calls=%async_computation.2 | async-start | bytes 524288 | tf_op jit(solution)/shard_map/all_to_all | solution.py:315
  347.5 14.0 %collective-permute-start.4 = (bf16[144,1024]{1,0:T(8,128)(2,1)S(1)}, bf16[144,1024]{1,0:T(8,128)(2,1)S(1)}, u32[]{:S(2)}, u32[]{:S(2)}) collective-permute-start(bf16[144,1024]{1,0:T(8,128)(2,1)S(1)} %get-tuple-element.121), channel_id=1, source_target_pairs={{0,2},{1,3},{2,0},{3,1},{4,6},{5,7},{6,4},{7,5},{8,10},{9,11},{10,... | collective-permute-start | bytes 884744 | tf_op jit(solution)/shard_map/ppermute | solution.py:476
  351.3 20.8 %all-to-all-start.4 = ((bf16[4,128,512]{1,2,0:T(8,128)(2,1)}), bf16[4,128,512]{1,2,0:T(8,128)(2,1)S(1)}, u32[]{:S(2)}, u32[]{:S(2)}) async-start(bf16[4,128,512]{1,2,0:T(8,128)(2,1)} %bitcast.26), calls=%async_computation.4 | async-start | bytes 1048576 | tf_op jit(solution)/shard_map/all_to_all | solution.py:315
  362.4 25.2 %collective-permute-start.5 = (bf16[2,144,1024]{2,1,0:T(8,128)(2,1)}, bf16[2,144,1024]{2,1,0:T(8,128)(2,1)S(1)}, u32[]{:S(2)}, u32[]{:S(2)}) collective-permute-start(bf16[2,144,1024]{2,1,0:T(8,128)(2,1)} %pad_maximum_fusion.7), channel_id=1, source_target_pairs={{0,1},{1,0},{2,3},{3,2},{4,5},{5,4},{6,7},{7,6},{8,9},{9,8},{10,11... | collective-permute-start | bytes 1769480 | tf_op jit(solution)/shard_map/ppermute | solution.py:478
  377.5 26.7 %all-to-all-start.6 = ((bf16[16,96,128]{2,1,0:T(8,128)(2,1)}), bf16[16,96,128]{2,1,0:T(8,128)(2,1)S(1)}, u32[]{:S(2)}, u32[]{:S(2)}) async-start(bf16[16,96,128]{2,1,0:T(8,128)(2,1)} %copy.165), calls=%async_computation.6 | async-start | bytes 786432 | tf_op jit(solution)/shard_map/all_to_all | solution.py:315
  404.2 42.8 %all-to-all-start.5 = ((bf16[4,144,1024]{2,1,0:T(8,128)(2,1)}), bf16[4,144,1024]{2,1,0:T(8,128)(2,1)S(1)}, u32[]{:S(2)}, u32[]{:S(2)}) async-start(bf16[4,144,1024]{2,1,0:T(8,128)(2,1)} %pad_maximum_fusion.2), calls=%async_computation.5 | async-start | bytes 2359296 | tf_op jit(solution)/shard_map/all_to_all | solution.py:315
  414.8 10.1 %collective-permute-start.7 = (bf16[64,3072]{1,0:T(8,128)(2,1)S(1)}, bf16[64,3072]{1,0:T(8,128)(2,1)S(1)}, u32[]{:S(2)}, u32[]{:S(2)}) collective-permute-start(bf16[64,3072]{1,0:T(8,128)(2,1)S(1)} %reshape.312), channel_id=1, source_target_pairs={{0,16},{16,0},{1,17},{17,1},{2,18},{18,2},{3,19},{19,3},{4,20},{20... | collective-permute-start | bytes 1179656 | tf_op jit(solution)/shard_map/ppermute | solution.py:306
  447.2 8.9 %collective-permute-start.6 = (bf16[144,1024]{1,0:T(8,128)(2,1)S(1)}, bf16[144,1024]{1,0:T(8,128)(2,1)S(1)}, u32[]{:S(2)}, u32[]{:S(2)}) collective-permute-start(bf16[144,1024]{1,0:T(8,128)(2,1)S(1)} %convert_element_type.161), channel_id=1, source_target_pairs={{0,16},{16,0},{1,17},{17,1},{2,18},{18,2},{3,19},{19,3},{4,20},{20... | collective-permute-start | bytes 884744 | tf_op jit(solution)/shard_map/ppermute | solution.py:306
  457.6 16.2 %collective-permute-start.8 = (bf16[64,5248]{1,0:T(8,128)(2,1)}, bf16[64,5248]{1,0:T(8,128)(2,1)S(1)}, u32[]{:S(2)}, u32[]{:S(2)}) collective-permute-start(bf16[64,5248]{1,0:T(8,128)(2,1)} %reduce-scatter.2.cloned.1.call-done), channel_id=1, source_target_pairs={{0,16},{16,0},{1,17},{17,1},{2,18},{18,2},{3,19},{19,3},{4,20},{20... | collective-permute-start | bytes 2015240 | tf_op jit(solution)/shard_map/ppermute | solution.py:306
  (25 other events, 85.9 us)
Sparse Core Ops, SparseCore 0:
  12.0 92.1 all-gather.3
  107.0 101.9 all-gather.5
  211.2 49.7 all-gather.7
  265.0 167.6 reduce-scatter.1
